TPU v7x, 32 devices: a whole 2x2x4 slice. The times are simulated.
32 devices in a mesh: seg: 8 (over z, y), row: 4 (over x, core).
Axes of the slice: x: 2, y: 2, z: 4, core: 2. Of those that a mesh axis runs over, the one named last changes fastest.
Arguments:
- left_env: float32 [8, 128, 6, 2048], P('seg', None, None, 'row'), may hold values from -4 to 4
- left_core: float32 [8, 2048, 2, 2048], P('seg', None, None, 'row'), may hold values from -0.125 to 0.125
- inv_sing: float32 [8, 2048], P('seg', 'row'), may hold values from 1 to 8
- mpo_pair: float32 [8, 2, 6, 6, 2, 2], P('seg'), may hold values from -1.75 to 1.75
- right_core: float32 [8, 2048, 2, 2048], P('seg', None, None, 'row'), may hold values from -0.125 to 0.125
- right_env: float32 [8, 6, 2048, 2048], P('seg', None, 'row'), may hold values from -0.078125 to 0.078125
Outputs:
- applied: float32 [8, 128, 2, 2, 2048], P('seg', None, None, None, 'row')
All inputs are finite; a program needn't handle non-finite values.
Results may differ from a plain program's by a relative error of at most 0.0003.
Values sent between devices are 32-bit elements; how exact they have to be, the bound alone decides.
No kernel may reach another device: no remote copies, remote signals or barrier semaphores. Data moves between devices by JAX's collectives and lax.ppermute only.
A program may use at most 192 MiB of HBM per device.

v0:
```python
import jax
import jax.numpy as jnp
from jax import lax
from jax.sharding import PartitionSpec as P


def from_behind(value, axis, steps):
    count = lax.axis_size(axis)
    initial, last = (max(0, -steps), min(count, count - steps))
    return lax.ppermute(value, axis, [(source, source + steps) for source in range(initial, last)])


def boundary(left_env, left_core, inv_sing, mpo_pair, right_core, right_env):
    high = lax.Precision.HIGHEST
    panel = left_env.shape[1]
    mpo_width = left_env.shape[2]
    bond = left_core.shape[1]
    cols = left_core.shape[3]
    core_a = left_core[0].reshape(bond, 2 * cols)
    core_b = right_core[0].reshape(bond, 2 * cols)
    piece = lax.all_gather(left_env, "row", axis=3, tiled=True)
    count = piece.shape[3]
    lefted = jnp.dot(
        piece.reshape(-1, count), core_a, precision=high, preferred_element_type=jnp.float32
    )
    scaled = lefted.reshape(1, panel, mpo_width, 2, cols) * inv_sing.reshape(1, 1, 1, 1, cols)
    piece = lax.all_gather(scaled, "row", axis=4, tiled=True)
    count = piece.shape[4]
    paired = jnp.dot(
        piece.reshape(-1, count), core_b, precision=high, preferred_element_type=jnp.float32
    )
    paired = paired.reshape(panel, mpo_width, 2, 2, cols)
    first = jnp.einsum("xyps,axstc->apytc", mpo_pair[0, 0], paired, precision=high)
    mixed = jnp.einsum("yzqt,apytc->apqzc", mpo_pair[0, 1], first, precision=high)
    term = jnp.dot(
        mixed.reshape(panel * 4, mpo_width * cols),
        right_env[0].reshape(mpo_width * cols, bond),
        precision=high,
        preferred_element_type=jnp.float32,
    )
    term = term.reshape(1, panel, 2, 2, bond)
    return lax.psum_scatter(term, "row", scatter_dimension=4, tiled=True)


def per_device(left_env, left_core, inv_sing, mpo_pair, right_core, right_env):
    core_next, env_next = from_behind((right_core, right_env), "seg", -1)
    result = boundary(left_env, left_core, inv_sing, mpo_pair, core_next, env_next)
    return result


def solution(mesh):
    return jax.shard_map(
        per_device,
        mesh=mesh,
        in_specs=(
            P("seg", None, None, "row"),
            P("seg", None, None, "row"),
            P("seg", "row"),
            P("seg", None, None, None, None, None),
            P("seg", None, None, "row"),
            P("seg", None, "row", None),
        ),
        out_specs=P("seg", None, None, None, "row"),
        check_vma=False,
    )
```

profile of v0, /device:TPU:0, one launch (start us, length us, event | category | flops | bytes accessed | tf_op | source)
XLA Modules:
  0.0 943.0 jit_solution(4739074005551734844)
XLA Ops:
  6.5 0.0 all-gather.4.cloned.1.call-start
  6.5 0.7 all-gather.4.cloned.1.call-update
  7.3 0.0 all-gather.6.cloned.1.call-start
  7.3 1.3 collective-permute-start.1
  8.6 8.7 copy.31
  17.3 12.3 %reshape.29 = f32[2,512,2048,1]{1,0,2,3:T(2,128)} reshape(f32[1024,2048]{0,1:T(8,128)} %bitcast.63) | data formatting | bytes 16777216 | tf_op jit(solution)/shard_map/dot_general | solution.py:23
  29.5 0.0 copy-start.1
  29.5 28.5 %all-gather.4.cloned.1.call-done = f32[1,128,6,2048]{3,1,2,0:T(8,128)} async-done(((f32[1,128,6,512]{3,1,2,0:T(8,128)}), f32[1,128,6,2048]{3,1,2,0:T(8,128)}) %all-gather.4.cloned.1.call-update) | async-done | bytes 6291472 | tf_op jit(solution)/shard_map/all_gather | solution.py:21
  58.0 25.1 %fusion.7 = f32[128,6,2,512]{3,0,2,1:T(8,128)S(1)} fusion(f32[2,512,2048,1]{1,0,2,3:T(2,128)} %reshape.29, f32[1,128,6,2048]{3,1,2,0:T(8,128)} %all-gather.4.cloned.1.call-done), kind=kOutput, calls=%fused_computation.7 | convolution fusion | flops 19327352832 | bytes 17825792 | tf_op jit(solution)/shard_map/dot_general | solution.py:23
  83.2 0.0 copy-start
  83.2 0.0 copy-done.1
  83.2 4.1 copy_multiply_fusion
  87.3 0.0 all-gather.6.cloned.1.call-update
  87.3 0.0 reduce-scatter.2.cloned.1.call-start
  87.3 1.3 collective-permute-start
  88.6 0.0 copy-done
  88.7 0.1 copy.30
  88.8 643.5 %collective-permute-done = f32[1,2048,2,512]{3,2,1,0:T(2,128)} collective-permute-done((f32[1,2048,2,512]{3,2,1,0:T(2,128)}, f32[1,2048,2,512]{3,2,1,0:T(2,128)}, u32[]{:S(2)}, u32[]{:S(2)}) %collective-permute-start) | collective-permute-done | bytes 8388640 | tf_op jit(solution)/shard_map/ppermute | solution.py:10
  732.2 8.8 copy.32
  741.0 11.7 %reshape.31 = f32[2,512,2048,1,1]{1,0,2,3,4:T(2,128)} reshape(f32[1024,2048]{0,1:T(8,128)} %bitcast.62) | data formatting | bytes 16777216 | tf_op jit(solution)/shard_map/dot_general | solution.py:29
  752.7 0.0 all-gather.6.cloned.1.call-done
  752.7 54.1 %fusion.13 = f32[128,6,2,2,512,1]{4,0,3,2,1,5:T(8,128)S(1)} fusion(f32[2,512,2048,1,1]{1,0,2,3,4:T(2,128)} %reshape.31, f32[128,6,2,2048,1]{3,2,1,0,4:T(2,128)} %bitcast.67), kind=kOutput, calls=%fused_computation.13 | convolution fusion | flops 38654705664 | bytes 27262976 | tf_op jit(solution)/shard_map/dot_general | solution.py:29
  806.9 14.3 %fusion.4 = f32[128,2,512,6,2,1]{2,3,5,1,4,0:T(8,128)S(1)} fusion(f32[128,6,2,2,512,1]{4,0,3,2,1,5:T(8,128)S(1)} %fusion.13, f32[6,6,2,2,1,1]{1,3,2,0,4,5:T(2,128)S(1)} %get-tuple-element.6), kind=kOutput, calls=%fused_computation.4 | convolution fusion | flops 226492416 | bytes 12583488 | tf_op jit(solution)/shard_map/xyps,axstc->apytc/dot_general | solution.py:33
  821.2 10.7 %fusion.10 = f32[128,2,2,6,512]{4,3,2,1,0:T(8,128)} fusion(f32[128,2,512,6,2,1]{2,3,5,1,4,0:T(8,128)S(1)} %fusion.4, f32[1,1,6,6,2,2]{2,3,5,4,1,0:T(8,128)S(1)} %copy.30), kind=kOutput, calls=%fused_computation.11 | convolution fusion | flops 226492416 | bytes 12583488 | tf_op jit(solution)/shard_map/yzqt,apytc->apqzc/dot_general | solution.py:34
  831.9 9.1 copy.11
  841.0 0.0 collective-permute-done.1
  841.0 46.2 %convolution_bitcast_fusion = f32[1,128,2,2,2048]{4,1,3,2,0:T(8,128)} fusion(f32[128,2,2,3072]{0,3,2,1:T(8,128)} %bitcast.65, f32[3072,2048,1,1]{1,0,3,2:T(8,128)} %bitcast.24), kind=kOutput, calls=%fused_computation.10 | convolution fusion | flops 38654705664 | bytes 35651584 | tf_op jit(solution)/shard_map/dot_general | solution.py:35
  887.2 0.0 reduce-scatter.2.cloned.1.call-update
  887.2 46.0 %reduce-scatter.2.cloned.1.call-done = f32[1,128,2,2,512]{4,1,3,2,0:T(8,128)} async-done(((f32[1,128,2,2,2048]{4,1,3,2,0:T(8,128)}), f32[1,128,2,2,512]{4,1,3,2,0:T(8,128)}) %reduce-scatter.2.cloned.1.call-update) | async-done | bytes 1048592 | tf_op jit(solution)/shard_map/reduce_scatter | solution.py:42
  933.2 3.0 copy.13
  (1 shorter events, 0.0 us)
Async XLA Ops:
  6.5 51.5 %all-gather.4.cloned.1.call-start = ((), (), s32[]{:S(2)}) async-start(), calls=%async_computation.1 | async-start | bytes 7864320 | tf_op jit(solution)/shard_map/all_gather | solution.py:21
  7.3 745.5 %all-gather.6.cloned.1.call-start = ((), (), s32[]{:S(2)}) async-start(), calls=%async_computation.3 | async-start | bytes 15728640 | tf_op jit(solution)/shard_map/all_gather | solution.py:27
  7.3 833.7 %collective-permute-start.1 = (f32[1,6,512,2048]{3,2,1,0:T(8,128)}, f32[1,6,512,2048]{3,2,1,0:T(8,128)}, u32[]{:S(2)}, u32[]{:S(2)}) collective-permute-start(f32[1,6,512,2048]{3,2,1,0:T(8,128)} %param.11), channel_id=1, source_target_pairs={{4,0},{8,4},{12,8},{16,12},{20,16},{24,20},{28,24},{5,1},{9,5},{13... | collective-permute-start | bytes 75497480 | tf_op jit(solution)/shard_map/ppermute | solution.py:10
  29.5 53.6 %copy-start.1 = (f32[1,512]{1,0:T(1,128)S(1)}, f32[1,512]{1,0:T(1,128)}, u32[]{:S(2)}) copy-start(f32[1,512]{1,0:T(1,128)} %param.8) | copy-start | bytes 6148
  83.2 5.5 copy-start
  87.3 845.9 %reduce-scatter.2.cloned.1.call-start = ((), (), s32[]{:S(2)}) async-start(), calls=%async_computation.2 | async-start | bytes 5242880 | tf_op jit(solution)/shard_map/reduce_scatter | solution.py:42
  87.3 644.9 %collective-permute-start = (f32[1,2048,2,512]{3,2,1,0:T(2,128)}, f32[1,2048,2,512]{3,2,1,0:T(2,128)}, u32[]{:S(2)}, u32[]{:S(2)}) collective-permute-start(f32[1,2048,2,512]{3,2,1,0:T(2,128)} %param.10), channel_id=1, source_target_pairs={{4,0},{8,4},{12,8},{16,12},{20,16},{24,20},{28,24},{5,1},{9,5},{13... | collective-permute-start | bytes 25165832 | tf_op jit(solution)/shard_map/ppermute | solution.py:10
Sparse Core Ops, SparseCore 0:
  8.9 49.0 all-gather.3
  87.4 83.7 all-gather.5
  887.3 45.8 reduce-scatter.1
where the time goes:
time: 946 us; the launch traced here: 943 us
  waiting for transfers between devices  719 us (76%)
  matrix products  150 us (16%)
  local copies, waits for them, and re-layouts  53.7 us (6%)
  between operations  13.5 us (1%)
    ppermute x2, waiting for transfers between devices, from_behind(): lax.ppermute(value, axis, [(source, source + steps) for source in range(i...  643 us
    dot_general x1, matrix products, boundary(): jnp.dot(piece.reshape(-1, count), core_b, precision=high, preferred_eleme...  54.1 us
    dot_general x1, matrix products, boundary(): jnp.dot(mixed.reshape(panel * 4, mpo_width * cols), right_env[0].reshape(...  46.2 us
    reduce_scatter x1, waiting for transfers between devices, boundary(): return lax.psum_scatter(term, 'row', scatter_dimension=4, tiled=True)  46 us
    all_gather x1, waiting for transfers between devices, boundary(): piece = lax.all_gather(left_env, 'row', axis=3, tiled=True)  28.5 us
    dot_general x1, matrix products, boundary(): jnp.dot(piece.reshape(-1, count), core_a, precision=high, preferred_eleme...  25.1 us
  transfers between devices with their start and end apart: 5, of which 3 were waited for; matrix products, arithmetic and copies ran while one was open for 17% of the time, Pallas kernels for 0%

commit v1 on v0

v1 whole, which is shorter than its diff:
```python
import jax
import jax.numpy as jnp
from jax import lax
from jax.experimental import pallas as pl
from jax.experimental.pallas import tpu as pltpu
from jax.sharding import PartitionSpec as P

MIB = 1024 * 1024
LANES = 128
WIDE = 256
SLOTS = 4
TOKEN = jax.ShapeDtypeStruct((8, LANES), jnp.float32)
COST = 2 * 10**9
SIZES = (32, 32, 32, 32)
FETCHES = (1, 1, 2)

def shifted(value, axis, steps):
    count = lax.axis_size(axis)
    first, last = (max(0, -steps), min(count, count - steps))
    return lax.ppermute(value, axis, [(source, source + steps) for source in range(first, last)])


def swapped(value, axis, bit):
    count = lax.axis_size(axis)
    return lax.ppermute(value, axis, [(source, source ^ bit) for source in range(count)])


def in_vmem(value):
    return pltpu.with_memory_space_constraint(value, pltpu.VMEM)


def in_hbm(value):
    return pltpu.with_memory_space_constraint(value, pltpu.HBM)


VMEM, SMEM, ANY = (
    pl.BlockSpec(memory_space=space) for space in (pltpu.VMEM, pltpu.SMEM, pl.ANY)
)


def run(name, vmem, after, *parts):
    inputs = [pair for part in parts for pair in part[1]]
    waits = len(after)
    outs = [shape for part in parts for shape in part[2]]
    groups = {id(part[3]): part[3] for part in parts}
    places = dict(zip(groups, [sum(map(len, list(groups.values())[:n])) for n in range(len(groups))]))
    scratch = [shape for group in groups.values() for shape in group]

    def kernel(*refs):
        refs = list(refs)
        ins, refs = refs[:len(inputs)], refs[len(inputs) + waits:]
        results, own = refs[:len(outs)], refs[len(outs):]
        for part in parts:
            taken = []
            for group, number in ((ins, len(part[1])), (results, len(part[2]))):
                taken += group[:number]
                del group[:number]
            place = places[id(part[3])]
            part[0](*taken, *own[place:place + len(part[3])])

    values = pl.pallas_call(
        kernel,
        in_specs=[spec for spec, _ in inputs] + [ANY] * waits,
        out_specs=[VMEM] * len(outs),
        out_shape=outs,
        scratch_shapes=scratch,
        compiler_params=pltpu.CompilerParams(vmem_limit_bytes=vmem * MIB),
        cost_estimate=pl.CostEstimate(flops=COST, bytes_accessed=0, transcendentals=0),
        name=name,
    )(*[value for _, value in inputs], *after)
    values = list(values)
    result = []
    for part in parts:
        result.append(values[:len(part[2])])
        del values[:len(part[2])]
    return result

def halves(x):
    hi = x.astype(jnp.bfloat16)
    lo = (x - hi.astype(jnp.float32)).astype(jnp.bfloat16)
    return hi, lo


def product(both, w_hi, w_lo):
    rows = both.shape[0] // 2
    wide = jnp.dot(both, w_hi, preferred_element_type=jnp.float32)
    return wide[:rows] + wide[rows:] + jnp.dot(
        both[:rows], w_lo, preferred_element_type=jnp.float32
    )


def streamed(x_hbm, buffers, sems, body):
    slots, block = buffers.shape[:2]
    steps = x_hbm.shape[0] // block

    def copy(t):
        slot = lax.rem(t, slots)
        rows = pl.ds(pl.multiple_of(t * block, block), block)
        return pltpu.make_async_copy(x_hbm.at[rows], buffers.at[slot], sems.at[slot])

    for t in range(slots - 1):
        copy(t).start()

    @pl.loop(0, steps)
    def _(t):
        @pl.when(t + slots - 1 < steps)
        def _():
            copy(t + slots - 1).start()

        copy(t).wait()
        body(t, buffers.at[lax.rem(t, slots)])


def split_core(core):
    bond, spins, cols = core.shape
    tiles = cols // LANES
    step = spins * tiles
    block = bond // 8
    flat = core.reshape(bond, spins, tiles, LANES).transpose(0, 2, 1, 3).reshape(bond * step, LANES)

    def body(x_hbm, hi_ref, lo_ref, token_ref, buffers, sems):
        def split(t, x_ref):
            rows = pl.ds(pl.multiple_of(t * block, block), block)
            for tile in range(tiles):
                lanes = slice(tile * LANES, (tile + 1) * LANES)
                for i in range(spins):
                    x = x_ref[pl.ds(tile * spins + i, block, stride=step), :]
                    hi_ref[i, rows, lanes], lo_ref[i, rows, lanes] = halves(x)

        streamed(x_hbm, buffers, sems, split)
        token_ref[...] = jnp.zeros_like(token_ref)

    out = pltpu.VMEM((spins, bond, cols), jnp.bfloat16)
    scratch = [
        pltpu.VMEM((SLOTS, block * step, LANES), jnp.float32),
        pltpu.SemaphoreType.DMA((SLOTS,)),
    ]
    return body, [(ANY, in_hbm(flat))], [out, out, TOKEN], scratch


def split_env(env):
    rows, cols = env.shape
    block = LANES

    def body(x_hbm, hi_ref, lo_ref, token_ref, buffers, sems):
        def split(t, x_ref):
            at = pl.ds(pl.multiple_of(t * block, block), block)
            hi_ref[at, :], lo_ref[at, :] = halves(x_ref[...])

        streamed(x_hbm, buffers, sems, split)
        token_ref[...] = jnp.zeros_like(token_ref)

    out = pltpu.VMEM((rows, cols), jnp.bfloat16)
    scratch = [
        pltpu.VMEM((SLOTS, block, cols), jnp.float32),
        pltpu.SemaphoreType.DMA((SLOTS,)),
    ]
    return body, [(ANY, in_hbm(env))], [out, out, TOKEN], scratch


def cut(env, start, size):
    width, _, cols = env.shape

    def body(env_hbm, out_ref, sem):
        copy = pltpu.make_async_copy(env_hbm.at[:, pl.ds(start, size), :], out_ref, sem)
        copy.start()
        copy.wait()

    out = pltpu.VMEM((width, size, cols), env.dtype)
    return body, [(ANY, in_hbm(env))], [out], [pltpu.SemaphoreType.DMA(())]


def copied(x):
    def body(x_ref, out_ref):
        out_ref[...] = x_ref[...]

    return body, [(VMEM, x)], [jax.ShapeDtypeStruct(x.shape, x.dtype)], []


def added(x, y):
    def body(x_ref, y_ref, out_ref):
        out_ref[...] = x_ref[...] + y_ref[...]

    return body, [(VMEM, x), (VMEM, y)], [jax.ShapeDtypeStruct(x.shape, x.dtype)], []


def lay_out(row, pieces, both_ref):
    rows = both_ref.shape[0] // 2
    for d, x in enumerate(pieces):
        cols = x.shape[-1]
        hi, lo = halves(x.reshape(rows, cols))
        at = pl.ds(pl.multiple_of((row ^ d) * cols, cols), cols)
        both_ref[:rows, at] = hi
        both_ref[rows:, at] = lo


def left(row, mpo, pieces, start, panel, core_hi, core_lo, inv):
    width, _, cols = pieces[0].shape
    spins, bond, _ = core_hi.shape
    count = len(pieces)
    wide = min(WIDE, cols)

    def body(row_ref, mpo_ref, *refs):
        pieces = refs[:count]
        hi_ref, lo_ref, inv_ref, out_ref, both_ref, acc_ref = refs[count:]
        lay_out(row_ref[0], [ref[:, start:start + panel, :] for ref in pieces], both_ref)

        @pl.loop(0, spins * (cols // wide))
        def _(n):
            i, at = n % spins, pl.ds(pl.multiple_of(n // spins * wide, wide), wide)
            acc_ref[i, :, at] = product(both_ref[...], hi_ref[i, :, at], lo_ref[i, :, at])

        for c in range(0, cols, wide):
            at = slice(c, c + wide)
            inv = inv_ref[:, at]
            for p in range(2):
                for y in range(width):
                    total = None
                    for w in range(width):
                        for i in range(spins):
                            scalar = mpo_ref[((w * width + y) * 2 + p) * 2 + i]
                            value = scalar * acc_ref[i, w * panel:(w + 1) * panel, at]
                            total = value if total is None else total + value
                    out_ref[p * width + y, :, at] = total * inv

    inputs = [(SMEM, row), (SMEM, mpo)] + [(VMEM, piece) for piece in pieces]
    inputs += [(VMEM, in_vmem(core_hi)), (VMEM, in_vmem(core_lo)), (VMEM, inv)]
    out = jax.ShapeDtypeStruct((2 * width, panel, cols), jnp.float32)
    scratch = [
        pltpu.VMEM((2 * width * panel, bond), jnp.bfloat16),
        pltpu.VMEM((spins, width * panel, cols), jnp.float32),
    ]
    return body, inputs, [out], scratch


def right(row, mpo, pieces, core_hi, core_lo, env_hi, env_lo):
    blocks, panel, cols = pieces[0].shape
    width = blocks // 2
    spins, bond, _ = core_hi.shape
    inner, outer = env_hi.shape
    count = len(pieces)
    half = count // 2
    out_cols = outer // count

    def body(row_ref, mpo_ref, *refs):
        pieces = refs[:count]
        core_hi, core_lo, env_hi, env_lo, send_ref, keep_ref = refs[count:count + 6]
        both_ref, first_ref, mixed_ref = refs[count + 6:]
        row = row_ref[0]
        lay_out(row, [ref[...] for ref in pieces], both_ref)
        wide = min(WIDE, cols)

        @pl.loop(0, spins * (cols // wide))
        def _(n):
            j, at = n % spins, pl.ds(pl.multiple_of(n // spins * wide, wide), wide)
            first_ref[j, :, at] = product(both_ref[...], core_hi[j, :, at], core_lo[j, :, at])

        for c in range(0, cols, wide):
            at = slice(c, c + wide)
            for p in range(2):
                for q in range(2):
                    to = (p * 2 + q) * panel
                    for z in range(width):
                        total = None
                        for y in range(width):
                            for j in range(spins):
                                scalar = mpo_ref[((y * width + z) * 2 + q) * 2 + j]
                                start = (p * width + y) * panel
                                value = scalar * first_ref[j, start:start + panel, at]
                                total = value if total is None else total + value
                        hi, lo = halves(total)
                        lanes = slice(z * cols + c, z * cols + c + wide)
                        mixed_ref[to:to + panel, lanes] = hi
                        mixed_ref[4 * panel + to:5 * panel + to, lanes] = lo
        narrow = min(WIDE, out_cols)
        for parity, out_ref in ((1, send_ref), (0, keep_ref)):

            @pl.loop(0, half * (out_cols // narrow))
            def _(n):
                m, c = n % half, pl.multiple_of(n // half * narrow, narrow)
                source = pl.multiple_of((row ^ (2 * m + parity)) * out_cols + c, narrow)
                at = pl.ds(source, narrow)
                out_ref[m, :, pl.ds(c, narrow)] = product(
                    mixed_ref[...], env_hi[:, at], env_lo[:, at]
                )

    inputs = [(SMEM, row), (SMEM, mpo)] + [(VMEM, piece) for piece in pieces]
    inputs += [(VMEM, in_vmem(value)) for value in (core_hi, core_lo, env_hi, env_lo)]
    out = jax.ShapeDtypeStruct((half, 4 * panel, out_cols), jnp.float32)
    scratch = [
        pltpu.VMEM((2 * blocks * panel, bond), jnp.bfloat16),
        pltpu.VMEM((spins, blocks * panel, cols), jnp.float32),
        pltpu.VMEM((8 * panel, inner), jnp.bfloat16),
    ]
    return body, inputs, [out, out], scratch


def reduced(send, keep, axis):
    came = swapped(send, axis, 1)
    sums = [(keep[m], came[m]) for m in range(keep.shape[0])]
    bit = 2
    while len(sums) > 1:
        came = [swapped(one + two, axis, bit) for one, two in sums[1::2]]
        sums = [(one + two, three) for (one, two), three in zip(sums[0::2], came)]
        bit *= 2
    return sums[0]


def per_device(left_env, left_core, inv_sing, mpo_pair, right_core, right_env):
    count = lax.axis_size("row")
    row = lax.axis_index("row").astype(jnp.int32).reshape(1)
    env = left_env[0].transpose(1, 0, 2)
    mpo_left = mpo_pair[0, 0].reshape(-1)
    mpo_right = shifted(mpo_pair[0, 1].reshape(-1), "seg", 1)
    flat_env = right_env[0].reshape(-1, right_env.shape[3])
    chunks = len(SIZES)

    begins = [sum(SIZES[:k]) for k in range(chunks)]
    firsts = [sum(FETCHES[:f]) for f in range(len(FETCHES))]
    fetched, spread = {}, {}

    def gathered(own, other, *after):
        if after:
            ((other,),) = run("copied", 4, after, copied(other))
        pieces = {0: own, count // 2: other}
        bit = count // 4
        while bit:
            for d in list(pieces):
                pieces[d ^ bit] = swapped(pieces[d], "row", bit)
            bit //= 2
        return [pieces[d] for d in range(count)]

    def fetch(f, *after):
        k, number = firsts[f], FETCHES[f]
        ((own,),) = run("cut", 2, after, cut(env, begins[k], sum(SIZES[k:k + number])))
        fetched[f] = own, swapped(own, "row", count // 2)

    def left_part(k, *after):
        f = max(f for f in range(len(FETCHES)) if firsts[f] <= k)
        if f not in spread:
            spread[f] = gathered(*fetched[f], *after)
        return left(
            row, mpo_left, spread[f], begins[k] - begins[firsts[f]], SIZES[k], *core_a, inv_sing
        )

    fetch(0)
    (((*core_a, token)),) = run("split_a", 10, [], split_core(left_core[0]))
    fetch(1, fetched[0][1], token)
    ((scaled,),) = run("left_0", 10, [mpo_right], left_part(0))
    sent, crossed, sums = {}, {}, {}

    def send_on(k, value):
        sent[k] = shifted(value, "seg", 1)

    def cross(k, *after):
        if after:
            ((sent[k],),) = run("copied", 4, after, copied(sent[k]))
        crossed[k] = swapped(sent[k], "row", count // 2)

    def right_part(k, *after):
        return right(row, mpo_right, gathered(sent[k], crossed[k], *after), *core_b, *env_b)

    send_on(0, scaled)
    fetch(2, fetched[1][1], scaled)
    part = left_part(1)
    (scaled,), (*core_b, token) = run("left_1", 14, [scaled], part, split_core(right_core[0]))
    send_on(1, scaled)
    cross(0)
    after = [scaled, token, sent[0], fetched[2][1]]
    parts = [left_part(k, scaled) for k in range(2, chunks)]
    largest = max(parts, key=lambda part: part[3][0].shape)[3]
    parts = [part[:3] + (largest,) if part[3][0].shape == largest[0].shape else part for part in parts]
    (*env_b, token), *rest = run("left_2", 13, after, split_env(flat_env), *parts)
    for k, (scaled,) in enumerate(rest, 2):
        send_on(k, scaled)
    cross(1, token)
    outs = []

    def give_back(first, last, *after):
        results = run("added", 4, after, *[added(*reduced(*sums[k], "row")) for k in range(first, last)])
        rows = jnp.concatenate([value for (value,) in results])
        rows = shifted(rows, "seg", -1)
        begin = 0
        for size in SIZES[first:last]:
            own = rows[begin:begin + 4 * size]
            begin += 4 * size
            outs.append(own.reshape(2, 2, size, own.shape[1]).transpose(2, 0, 1, 3))
        return rows

    for k in range(chunks):
        if k == chunks - 1:
            early = give_back(0, chunks - 3)
        after = [token if k == 0 else send]
        part = right_part(k, *after)
        ((send, keep),) = run(f"right_{k}", 15, after, part)
        sums[k] = send, keep
        if k + 2 < chunks:
            cross(k + 2, send)
    give_back(chunks - 3, chunks - 1, early, send)
    give_back(chunks - 1, chunks)
    return jnp.concatenate(outs, 0)[None]


def solution(mesh):
    return jax.shard_map(
        per_device,
        mesh=mesh,
        in_specs=(
            P("seg", None, None, "row"),
            P("seg", None, None, "row"),
            P("seg", "row"),
            P("seg", None, None, None, None, None),
            P("seg", None, None, "row"),
            P("seg", None, "row", None),
        ),
        out_specs=P("seg", None, None, None, "row"),
        check_vma=False,
    )
```

time: 946 us -> 193 us (0.20)
  waiting for transfers between devices: 719 us -> 37.8 us
  matrix products: 150 us -> 0 us
  Pallas kernels: 0 us -> 98.1 us
  local copies, waits for them, and re-layouts: 53.7 us -> 11 us
  starting transfers between devices: 2.67 us -> 43.7 us
  between operations: 13.5 us -> 0.52 us
    ppermute x2 -> x37, waiting for transfers between devices: 643 us -> 37.8 us  [the longest x29 21.6 us: swapped(): lax.ppermute(value, axis, [(source, source ^ bit) for source in range(cou...]
    dot_general x5 -> x0, matrix products: 150 us -> none  [the longest x1 54.1 us: boundary(): jnp.dot(piece.reshape(-1, count), core_b, precision=high, preferred_eleme...]
    pallas_call x0 -> x22, Pallas kernels: none -> 98.1 us  [run(): pl.pallas_call(kernel, in_specs=[spec for spec, _ in inputs] + [ANY] * wa...]
    reduce_scatter x1 -> x0, waiting for transfers between devices: 46 us -> none  [boundary(): return lax.psum_scatter(term, 'row', scatter_dimension=4, tiled=True)]
    ppermute x2 -> x37, starting transfers between devices: 2.58 us -> 43.7 us  [the longest x8 26 us: shifted(): lax.ppermute(value, axis, [(source, source + steps) for source in range(f...]
    all_gather x2 -> x0, waiting for transfers between devices: 28.5 us -> none  [the longest x1 28.5 us: boundary(): piece = lax.all_gather(left_env, 'row', axis=3, tiled=True)]
    dot_general x2 -> x0, local copies, waits for them, and re-layouts: 24 us -> none  [the longest x1 12.3 us: boundary(): jnp.dot(piece.reshape(-1, count), core_a, precision=high, preferred_eleme...]
  transfers between devices with their start and end apart: 5 -> 37, of which waited for: 3 -> 12; matrix products, arithmetic and copies ran while one was open for 17% -> 1% of each run, Pallas kernels for 0% -> 50%
where the time goes in v1:
time: 193 us
  Pallas kernels  98.1 us (51%)
  starting transfers between devices  43.7 us (23%)
  waiting for transfers between devices  37.8 us (20%)
  local copies, waits for them, and re-layouts  11 us (6%)
    pallas_call x22, Pallas kernels, run(): pl.pallas_call(kernel, in_specs=[spec for spec, _ in inputs] + [ANY] * wa...  98.1 us
    ppermute x8, starting transfers between devices, shifted(): lax.ppermute(value, axis, [(source, source + steps) for source in range(f...  26 us
    ppermute x29, waiting for transfers between devices, swapped(): lax.ppermute(value, axis, [(source, source ^ bit) for source in range(cou...  21.6 us
    ppermute x29, starting transfers between devices, swapped(): lax.ppermute(value, axis, [(source, source ^ bit) for source in range(cou...  17.7 us
    ppermute x8, waiting for transfers between devices, shifted(): lax.ppermute(value, axis, [(source, source + steps) for source in range(f...  16.2 us
    unnamed x18, local copies, waits for them, and re-layouts  9.49 us
  transfers between devices with their start and end apart: 37, of which 12 were waited for; matrix products, arithmetic and copies ran while one was open for 1% of the time, Pallas kernels for 50%

profile of v1, /device:TPU:0, one launch (start us, length us, event | category | flops | bytes accessed | tf_op | source)
XLA Modules:
  0.0 192.8 jit_solution(16898765372727087496)
XLA Ops:
  0.0 1.0 cut.3.refs_2_
  1.0 3.0 %collective-permute-start.2 = (f32[6,32,512]{2,1,0:T(8,128)S(1)}, f32[6,32,512]{2,1,0:T(8,128)S(1)}, u32[]{:S(2)}, u32[]{:S(2)}) collective-permute-start(f32[6,32,512]{2,1,0:T(8,128)S(1)} %cut.3.refs_2_), channel_id=1, source_target_pairs={{0,2},{1,3},{2,0},{3,1},{4,6},{5,7},{6,4},{7,5},{8,10},{9,11},{10,... | collective-permute-start | bytes 1179656 | tf_op jit(solution)/shard_map/ppermute | solution.py:25
  4.0 4.3 %split_a.1 = (bf16[2,2048,512]{2,1,0:T(8,128)(2,1)S(1)}, bf16[2,2048,512]{2,1,0:T(8,128)(2,1)S(1)}, f32[8,128]{1,0:T(8,128)S(1)}) custom-call(f32[16384,128]{1,0:T(8,128)} %bitcast.49), custom_call_target="tpu_custom_call" | custom-call | flops 2000000000 | tf_op jit(solution)/shard_map/split_a/pallas_call | solution.py:61
  8.4 2.0 %copy-done = bf16[2,2048,512]{2,1,0:T(8,128)(2,1)} copy-done((bf16[2,2048,512]{2,1,0:T(8,128)(2,1)}, bf16[2,2048,512]{2,1,0:T(8,128)(2,1)S(1)}, u32[]{:S(2)}) %copy-start) | copy-done | bytes 4194328
  10.4 2.0 %copy-done.3 = bf16[2,2048,512]{2,1,0:T(8,128)(2,1)} copy-done((bf16[2,2048,512]{2,1,0:T(8,128)(2,1)}, bf16[2,2048,512]{2,1,0:T(8,128)(2,1)S(1)}, u32[]{:S(2)}) %copy-start.3) | copy-done | bytes 4194328
  12.3 0.8 collective-permute-done.2.refs_4_.refs_1_
  13.2 1.0 cut.4.refs_2_
  14.2 1.8 collective-permute-start.7
  16.3 3.4 %collective-permute-start = (f32[144]{0:T(256)S(1)}, f32[144]{0:T(256)S(1)}, u32[]{:S(2)}, u32[]{:S(2)}) collective-permute-start(f32[144]{0:T(256)S(1)} %reshape_squeeze.15), channel_id=1, source_target_pairs={{0,4},{4,8},{8,12},{12,16},{16,20},{20,24},{24,28},{1,5},{5,9},{9,... | collective-permute-start | bytes 1736 | tf_op jit(solution)/shard_map/ppermute | solution.py:20
  20.0 1.0 collective-permute-done.refs_9_.refs_1_
  21.0 2.2 %copy-done.1 = bf16[2,2048,512]{2,1,0:T(8,128)(2,1)S(1)} copy-done((bf16[2,2048,512]{2,1,0:T(8,128)(2,1)S(1)}, bf16[2,2048,512]{2,1,0:T(8,128)(2,1)}, u32[]{:S(2)}) %copy-start.1) | copy-done | bytes 4194328
  23.2 2.2 %copy-done.4 = bf16[2,2048,512]{2,1,0:T(8,128)(2,1)S(1)} copy-done((bf16[2,2048,512]{2,1,0:T(8,128)(2,1)S(1)}, bf16[2,2048,512]{2,1,0:T(8,128)(2,1)}, u32[]{:S(2)}) %copy-start.4) | copy-done | bytes 4194328
  25.4 4.7 %left_0.1.refs_2_.refs_10_ = f32[12,32,512]{2,1,0:T(8,128)S(1)} custom-call(s32[1]{0:T(128)} %bitcast.refs_0_.refs_1_.refs_10_, f32[144]{0:T(256)S(1)} %reshape_squeeze.16.refs_1_.refs_2_.refs_11_, f32[6,32,512]{2,1,0:T(8,128)S(1)} %cut.3.refs_2_, f32[6,32,512]{2,1,0:T(8,128)S(1)} %collective-permute-done.1.refs_3_, ...), custom_call_target="tpu_custom_call" | custom-call | flops 2000000000 | tf_op jit(solution)/shard_map/left_0/pallas_call | solution.py:61
  30.1 1.1 cut.5.refs_3_.refs_12_
  31.2 0.6 collective-permute-start.9
  32.4 4.2 %collective-permute-start.4 = (f32[12,32,512]{2,1,0:T(8,128)S(1)}, f32[12,32,512]{2,1,0:T(8,128)S(1)}, u32[]{:S(2)}, u32[]{:S(2)}) collective-permute-start(f32[12,32,512]{2,1,0:T(8,128)S(1)} %left_0.1.refs_2_.refs_10_), channel_id=1, source_target_pairs={{0,4},{4,8},{8,12},{12,16},{16,20},{20,24},{24,28},{1,5},{5,9},{9,... | collective-permute-start | bytes 2359304 | tf_op jit(solution)/shard_map/ppermute | solution.py:20
  36.7 8.2 %left_1.1 = (f32[12,32,512]{2,1,0:T(8,128)S(1)}, bf16[2,2048,512]{2,1,0:T(8,128)(2,1)S(1)}, bf16[2,2048,512]{2,1,0:T(8,128)(2,1)S(1)}, f32[8,128]{1,0:T(8,128)S(1)}) custom-call(s32[1]{0:T(128)} %bitcast.refs_0_.refs_1_.refs_10_, f32[144]{0:T(256)S(1)} %reshape_squeeze.16.refs_1_.refs_2_.refs_11_, f32[6,32,512]{2,1,0:T(8,128)S(1)} %cut.4.refs_2_, ...), custom_call_target="tpu_custom_call" | custom-call | flops 2000000000 | tf_op jit(solution)/shard_map/left_1/pallas_call | solution.py:61
  44.9 5.2 %collective-permute-done.9.refs_0_.refs_22_ = f32[6,64,512]{2,1,0:T(8,128)S(1)} collective-permute-done((f32[6,64,512]{2,1,0:T(8,128)S(1)}, f32[6,64,512]{2,1,0:T(8,128)S(1)}, u32[]{:S(2)}, u32[]{:S(2)}) %collective-permute-start.9) | collective-permute-done | bytes 786464 | tf_op jit(solution)/shard_map/ppermute | solution.py:25
  50.3 3.2 %collective-permute-done.4.refs_21_.refs_2_ = f32[12,32,512]{2,1,0:T(8,128)S(1)} collective-permute-done((f32[12,32,512]{2,1,0:T(8,128)S(1)}, f32[12,32,512]{2,1,0:T(8,128)S(1)}, u32[]{:S(2)}, u32[]{:S(2)}) %collective-permute-start.4) | collective-permute-done | bytes 786464 | tf_op jit(solution)/shard_map/ppermute | solution.py:20
  53.5 1.5 collective-permute-start.6
  55.0 4.4 %collective-permute-start.17 = (f32[12,32,512]{2,1,0:T(8,128)S(1)}, f32[12,32,512]{2,1,0:T(8,128)S(1)}, u32[]{:S(2)}, u32[]{:S(2)}) collective-permute-start(f32[12,32,512]{2,1,0:T(8,128)S(1)} %get-tuple-element.30.refs_1_.refs_19_), channel_id=1, source_target_pairs={{0,4},{4,8},{8,12},{12,16},{16,20},{20,24},{24,28},{1,5},{5,9},{9,... | collective-permute-start | bytes 2359304 | tf_op jit(solution)/shard_map/ppermute | solution.py:20
  59.5 1.1 copy-done.6
  60.6 19.0 %left_2.1 = (bf16[3072,2048]{1,0:T(8,128)(2,1)S(1)}, bf16[3072,2048]{1,0:T(8,128)(2,1)S(1)}, f32[8,128]{1,0:T(8,128)S(1)}, f32[12,32,512]{2,1,0:T(8,128)S(1)}, f32[12,32,512]{2,1,0:T(8,128)S(1)}) custom-call(f32[3072,2048]{1,0:T(8,128)} %bitcast.48, s32[1]{0:T(128)} %bitcast.refs_0_.refs_1_.refs_10_, f32[144]{0:T(256)S(1)} %reshape_squeeze.16.refs_1_.refs_2_.refs_11_, ...), custom_call_target="tpu_custom_call" | custom-call | flops 2000000000 | tf_op jit(solution)/shard_map/left_2/pallas_call | solution.py:61
  79.7 0.5 collective-permute-start.13
  80.3 0.6 collective-permute-start.19
  80.9 5.4 %collective-permute-start.23 = (f32[12,32,512]{2,1,0:T(8,128)S(1)}, f32[12,32,512]{2,1,0:T(8,128)S(1)}, u32[]{:S(2)}, u32[]{:S(2)}) collective-permute-start(f32[12,32,512]{2,1,0:T(8,128)S(1)} %get-tuple-element.41), channel_id=1, source_target_pairs={{0,4},{4,8},{8,12},{12,16},{16,20},{20,24},{24,28},{1,5},{5,9},{9,... | collective-permute-start | bytes 2359304 | tf_op jit(solution)/shard_map/ppermute | solution.py:20
  86.4 14.5 %right_0.1 = (f32[2,128,512]{2,1,0:T(8,128)S(1)}, f32[2,128,512]{2,1,0:T(8,128)S(1)}) custom-call(s32[1]{0:T(128)} %bitcast.refs_0_.refs_1_.refs_10_, f32[144]{0:T(256)S(1)} %collective-permute-done.refs_9_.refs_1_, f32[12,32,512]{2,1,0:T(8,128)S(1)} %collective-permute-done.4.refs_21_.refs_2_, f32[12,32,512]{2,1,0:T(8,128)S(1)} %collective-permute-done.5.refs_3_, ...), custom_call_target="tpu_custom_call" | custom-call | flops 2000000000 | tf_op jit(solution)/shard_map/right_0/pallas_call | solution.py:61
  101.0 0.5 collective-permute-start.20
  101.6 1.2 collective-permute-done.23.refs_0_
  102.8 1.6 collective-permute-start.25
  104.4 4.4 %collective-permute-start.29 = (f32[12,32,512]{2,1,0:T(8,128)S(1)}, f32[12,32,512]{2,1,0:T(8,128)S(1)}, u32[]{:S(2)}, u32[]{:S(2)}) collective-permute-start(f32[12,32,512]{2,1,0:T(8,128)S(1)} %get-tuple-element.44), channel_id=1, source_target_pairs={{0,4},{4,8},{8,12},{12,16},{16,20},{20,24},{24,28},{1,5},{5,9},{9,... | collective-permute-start | bytes 2359304 | tf_op jit(solution)/shard_map/ppermute | solution.py:20
  109.4 14.5 %right_1.1 = (f32[2,128,512]{2,1,0:T(8,128)S(1)}, f32[2,128,512]{2,1,0:T(8,128)S(1)}) custom-call(s32[1]{0:T(128)} %bitcast.refs_0_.refs_1_.refs_10_, f32[144]{0:T(256)S(1)} %collective-permute-done.refs_9_.refs_1_, f32[12,32,512]{2,1,0:T(8,128)S(1)} %copied.10.refs_2_, f32[12,32,512]{2,1,0:T(8,128)S(1)} %collective-permute-done.18.refs_3_, ...), custom_call_target="tpu_custom_call" | custom-call | flops 2000000000 | tf_op jit(solution)/shard_map/right_1/pallas_call | solution.py:61
  124.4 0.6 collective-permute-start.31
  125.1 1.6 collective-permute-start.15
  127.1 14.5 %right_2.1 = (f32[2,128,512]{2,1,0:T(8,128)S(1)}, f32[2,128,512]{2,1,0:T(8,128)S(1)}) custom-call(s32[1]{0:T(128)} %bitcast.refs_0_.refs_1_.refs_10_, f32[144]{0:T(256)S(1)} %collective-permute-done.refs_9_.refs_1_, f32[12,32,512]{2,1,0:T(8,128)S(1)} %copied.12.refs_2_, f32[12,32,512]{2,1,0:T(8,128)S(1)} %collective-permute-done.24.refs_3_, ...), custom_call_target="tpu_custom_call" | custom-call | flops 2000000000 | tf_op jit(solution)/shard_map/right_2/pallas_call | solution.py:61
  141.7 3.1 %collective-permute-done.31.refs_0_ = f32[12,32,512]{2,1,0:T(8,128)S(1)} collective-permute-done((f32[12,32,512]{2,1,0:T(8,128)S(1)}, f32[12,32,512]{2,1,0:T(8,128)S(1)}, u32[]{:S(2)}, u32[]{:S(2)}) %collective-permute-start.31) | collective-permute-done | bytes 786464 | tf_op jit(solution)/shard_map/ppermute | solution.py:25
  145.4 4.4 %collective-permute-done.15.refs_1_ = f32[128,512]{1,0:T(8,128)S(1)} collective-permute-done((f32[128,512]{1,0:T(8,128)S(1)}, f32[128,512]{1,0:T(8,128)S(1)}, u32[]{:S(2)}, u32[]{:S(2)}) %collective-permute-start.15) | collective-permute-done | bytes 262176 | tf_op jit(solution)/shard_map/ppermute | solution.py:25
  149.8 1.5 collective-permute-start.16
  151.4 0.6 collective-permute-start.22
  152.1 1.6 collective-permute-start.28
  153.7 14.5 %right_3.1 = (f32[2,128,512]{2,1,0:T(8,128)S(1)}, f32[2,128,512]{2,1,0:T(8,128)S(1)}) custom-call(s32[1]{0:T(128)} %bitcast.refs_0_.refs_1_.refs_10_, f32[144]{0:T(256)S(1)} %collective-permute-done.refs_9_.refs_1_, f32[12,32,512]{2,1,0:T(8,128)S(1)} %copied.14.refs_2_, f32[12,32,512]{2,1,0:T(8,128)S(1)} %collective-permute-done.30.refs_3_, ...), custom_call_target="tpu_custom_call" | custom-call | flops 2000000000 | tf_op jit(solution)/shard_map/right_3/pallas_call | solution.py:61
  168.5 1.3 collective-permute-start.33
  170.3 0.6 collective-permute-start.35
  171.1 7.6 %collective-permute-done.35.refs_1_ = f32[128,512]{1,0:T(8,128)S(1)} collective-permute-done((f32[128,512]{1,0:T(8,128)S(1)}, f32[128,512]{1,0:T(8,128)S(1)}, u32[]{:S(2)}, u32[]{:S(2)}) %collective-permute-start.35) | collective-permute-done | bytes 262176 | tf_op jit(solution)/shard_map/ppermute | solution.py:25
  178.8 1.3 collective-permute-start.36
  180.1 5.7 %collective-permute-done.33 = f32[256,512]{1,0:T(8,128)S(1)} collective-permute-done((f32[256,512]{1,0:T(8,128)S(1)}, f32[256,512]{1,0:T(8,128)S(1)}, u32[]{:S(2)}, u32[]{:S(2)}) %collective-permute-start.33) | collective-permute-done | bytes 524320 | tf_op jit(solution)/shard_map/ppermute | solution.py:20
  186.2 5.0 %collective-permute-done.36 = f32[128,512]{1,0:T(8,128)S(1)} collective-permute-done((f32[128,512]{1,0:T(8,128)S(1)}, f32[128,512]{1,0:T(8,128)S(1)}, u32[]{:S(2)}, u32[]{:S(2)}) %collective-permute-start.36) | collective-permute-done | bytes 262176 | tf_op jit(solution)/shard_map/ppermute | solution.py:20
  191.4 1.4 maximum_bitcast_fusion
  (81 shorter events, 5.7 us)
Async XLA Ops:
  1.0 15.0 %copy-start.8 = (f32[1,2,6,6,2,2]{3,5,4,2,1,0:T(2,128)S(1)}, f32[1,2,6,6,2,2]{3,5,4,2,1,0:T(2,128)}, u32[]{:S(2)}) copy-start(f32[1,2,6,6,2,2]{3,5,4,2,1,0:T(2,128)} %param.9) | copy-start | bytes 3460
  1.0 20.0 %copy-start.7 = (f32[1,512]{1,0:T(1,128)S(1)}, f32[1,512]{1,0:T(1,128)}, u32[]{:S(2)}) copy-start(f32[1,512]{1,0:T(1,128)} %refs_18_.1) | copy-start | bytes 6148
  1.0 12.1 %collective-permute-start.2 = (f32[6,32,512]{2,1,0:T(8,128)S(1)}, f32[6,32,512]{2,1,0:T(8,128)S(1)}, u32[]{:S(2)}, u32[]{:S(2)}) collective-permute-start(f32[6,32,512]{2,1,0:T(8,128)S(1)} %cut.3.refs_2_), channel_id=1, source_target_pairs={{0,2},{1,3},{2,0},{3,1},{4,6},{5,7},{6,4},{7,5},{8,10},{9,11},{10,... | collective-permute-start | bytes 1179656 | tf_op jit(solution)/shard_map/ppermute | solution.py:25
  4.0 17.0 %collective-permute-start.1 = (f32[6,32,512]{2,1,0:T(8,128)S(1)}, f32[6,32,512]{2,1,0:T(8,128)S(1)}, u32[]{:S(2)}, u32[]{:S(2)}) collective-permute-start(f32[6,32,512]{2,1,0:T(8,128)S(1)} %cut.3.refs_2_), channel_id=1, source_target_pairs={{0,1},{1,0},{2,3},{3,2},{4,5},{5,4},{6,7},{7,6},{8,9},{9,8},{10,11... | collective-permute-start | bytes 1179656 | tf_op jit(solution)/shard_map/ppermute | solution.py:25
  8.4 2.0 %copy-start = (bf16[2,2048,512]{2,1,0:T(8,128)(2,1)}, bf16[2,2048,512]{2,1,0:T(8,128)(2,1)S(1)}, u32[]{:S(2)}) copy-start(bf16[2,2048,512]{2,1,0:T(8,128)(2,1)S(1)} %get-tuple-element.27.refs_6_.refs_7_.refs_16_) | copy-start | bytes 12582916
  10.4 2.0 %copy-start.3 = (bf16[2,2048,512]{2,1,0:T(8,128)(2,1)}, bf16[2,2048,512]{2,1,0:T(8,128)(2,1)S(1)}, u32[]{:S(2)}) copy-start(bf16[2,2048,512]{2,1,0:T(8,128)(2,1)S(1)} %get-tuple-element.28.refs_7_.refs_8_.refs_17_) | copy-start | bytes 12582916
  13.2 7.9 %collective-permute-start.3 = (f32[6,32,512]{2,1,0:T(8,128)S(1)}, f32[6,32,512]{2,1,0:T(8,128)S(1)}, u32[]{:S(2)}, u32[]{:S(2)}) collective-permute-start(f32[6,32,512]{2,1,0:T(8,128)S(1)} %collective-permute-done.2.refs_4_.refs_1_), channel_id=1, source_target_pairs={{0,1},{1,0},{2,3},{3,2},{4,5},{5,4},{6,7},{7,6},{8,9},{9,8},{10,11... | collective-permute-start | bytes 1179656 | tf_op jit(solution)/shard_map/ppermute | solution.py:25
  14.2 15.9 %collective-permute-start.7 = (f32[6,32,512]{2,1,0:T(8,128)S(1)}, f32[6,32,512]{2,1,0:T(8,128)S(1)}, u32[]{:S(2)}, u32[]{:S(2)}) collective-permute-start(f32[6,32,512]{2,1,0:T(8,128)S(1)} %cut.4.refs_2_), channel_id=1, source_target_pairs={{0,2},{1,3},{2,0},{3,1},{4,6},{5,7},{6,4},{7,5},{8,10},{9,11},{10,... | collective-permute-start | bytes 1179656 | tf_op jit(solution)/shard_map/ppermute | solution.py:25
  16.3 4.7 %collective-permute-start = (f32[144]{0:T(256)S(1)}, f32[144]{0:T(256)S(1)}, u32[]{:S(2)}, u32[]{:S(2)}) collective-permute-start(f32[144]{0:T(256)S(1)} %reshape_squeeze.15), channel_id=1, source_target_pairs={{0,4},{4,8},{8,12},{12,16},{16,20},{20,24},{24,28},{1,5},{5,9},{9,... | collective-permute-start | bytes 1736 | tf_op jit(solution)/shard_map/ppermute | solution.py:20
  21.0 2.2 %copy-start.1 = (bf16[2,2048,512]{2,1,0:T(8,128)(2,1)S(1)}, bf16[2,2048,512]{2,1,0:T(8,128)(2,1)}, u32[]{:S(2)}) copy-start(bf16[2,2048,512]{2,1,0:T(8,128)(2,1)} %copy-done) | copy-start | bytes 12582916
  23.2 2.2 %copy-start.4 = (bf16[2,2048,512]{2,1,0:T(8,128)(2,1)S(1)}, bf16[2,2048,512]{2,1,0:T(8,128)(2,1)}, u32[]{:S(2)}) copy-start(bf16[2,2048,512]{2,1,0:T(8,128)(2,1)} %copy-done.3) | copy-start | bytes 12582916
  25.4 11.3 %copy-start.2 = (bf16[2,2048,512]{2,1,0:T(8,128)(2,1)S(1)}, bf16[2,2048,512]{2,1,0:T(8,128)(2,1)}, u32[]{:S(2)}) copy-start(bf16[2,2048,512]{2,1,0:T(8,128)(2,1)} %copy-done) | copy-start | bytes 12582916
  31.2 18.9 %collective-permute-start.9 = (f32[6,64,512]{2,1,0:T(8,128)S(1)}, f32[6,64,512]{2,1,0:T(8,128)S(1)}, u32[]{:S(2)}, u32[]{:S(2)}) collective-permute-start(f32[6,64,512]{2,1,0:T(8,128)S(1)} %cut.5.refs_3_.refs_12_), channel_id=1, source_target_pairs={{0,2},{1,3},{2,0},{3,1},{4,6},{5,7},{6,4},{7,5},{8,10},{9,11},{10,... | collective-permute-start | bytes 2359304 | tf_op jit(solution)/shard_map/ppermute | solution.py:25
  31.8 4.8 %collective-permute-start.10 = (f32[6,32,512]{2,1,0:T(8,128)S(1)}, f32[6,32,512]{2,1,0:T(8,128)S(1)}, u32[]{:S(2)}, u32[]{:S(2)}) collective-permute-start(f32[6,32,512]{2,1,0:T(8,128)S(1)} %cut.4.refs_2_), channel_id=1, source_target_pairs={{0,1},{1,0},{2,3},{3,2},{4,5},{5,4},{6,7},{7,6},{8,9},{9,8},{10,11... | collective-permute-start | bytes 1179656 | tf_op jit(solution)/shard_map/ppermute | solution.py:25
  31.9 4.8 %collective-permute-start.11 = (f32[6,32,512]{2,1,0:T(8,128)S(1)}, f32[6,32,512]{2,1,0:T(8,128)S(1)}, u32[]{:S(2)}, u32[]{:S(2)}) collective-permute-start(f32[6,32,512]{2,1,0:T(8,128)S(1)} %collective-permute-done.7.refs_1_.refs_4_), channel_id=1, source_target_pairs={{0,1},{1,0},{2,3},{3,2},{4,5},{5,4},{6,7},{7,6},{8,9},{9,8},{10,11... | collective-permute-start | bytes 1179656 | tf_op jit(solution)/shard_map/ppermute | solution.py:25
  32.4 21.1 %collective-permute-start.4 = (f32[12,32,512]{2,1,0:T(8,128)S(1)}, f32[12,32,512]{2,1,0:T(8,128)S(1)}, u32[]{:S(2)}, u32[]{:S(2)}) collective-permute-start(f32[12,32,512]{2,1,0:T(8,128)S(1)} %left_0.1.refs_2_.refs_10_), channel_id=1, source_target_pairs={{0,4},{4,8},{8,12},{12,16},{16,20},{20,24},{24,28},{1,5},{5,9},{9,... | collective-permute-start | bytes 2359304 | tf_op jit(solution)/shard_map/ppermute | solution.py:20
  36.6 22.9 %collective-permute-start.8 = (f32[6,64,512]{2,1,0:T(8,128)S(1)}, f32[6,64,512]{2,1,0:T(8,128)S(1)}, u32[]{:S(2)}, u32[]{:S(2)}) collective-permute-start(f32[6,64,512]{2,1,0:T(8,128)S(1)} %cut.5.refs_3_.refs_12_), channel_id=1, source_target_pairs={{0,1},{1,0},{2,3},{3,2},{4,5},{5,4},{6,7},{7,6},{8,9},{9,8},{10,11... | collective-permute-start | bytes 2359304 | tf_op jit(solution)/shard_map/ppermute | solution.py:25
  50.1 9.4 %copy-start.5 = (f32[6,64,512]{2,1,0:T(8,128)}, f32[6,64,512]{2,1,0:T(8,128)S(1)}, u32[]{:S(2)}) copy-start(f32[6,64,512]{2,1,0:T(8,128)S(1)} %collective-permute-done.9.refs_0_.refs_22_) | copy-start | bytes 2359300
  50.2 9.3 %collective-permute-start.12 = (f32[6,64,512]{2,1,0:T(8,128)S(1)}, f32[6,64,512]{2,1,0:T(8,128)S(1)}, u32[]{:S(2)}, u32[]{:S(2)}) collective-permute-start(f32[6,64,512]{2,1,0:T(8,128)S(1)} %copied.8.refs_5_.refs_14_), channel_id=1, source_target_pairs={{0,1},{1,0},{2,3},{3,2},{4,5},{5,4},{6,7},{7,6},{8,9},{9,8},{10,11... | collective-permute-start | bytes 2359304 | tf_op jit(solution)/shard_map/ppermute | solution.py:25
  53.5 26.2 %collective-permute-start.6 = (f32[12,32,512]{2,1,0:T(8,128)S(1)}, f32[12,32,512]{2,1,0:T(8,128)S(1)}, u32[]{:S(2)}, u32[]{:S(2)}) collective-permute-start(f32[12,32,512]{2,1,0:T(8,128)S(1)} %collective-permute-done.4.refs_21_.refs_2_), channel_id=1, source_target_pairs={{0,2},{1,3},{2,0},{3,1},{4,6},{5,7},{6,4},{7,5},{8,10},{9,11},{10,... | collective-permute-start | bytes 2359304 | tf_op jit(solution)/shard_map/ppermute | solution.py:25
  55.0 25.3 %collective-permute-start.17 = (f32[12,32,512]{2,1,0:T(8,128)S(1)}, f32[12,32,512]{2,1,0:T(8,128)S(1)}, u32[]{:S(2)}, u32[]{:S(2)}) collective-permute-start(f32[12,32,512]{2,1,0:T(8,128)S(1)} %get-tuple-element.30.refs_1_.refs_19_), channel_id=1, source_target_pairs={{0,4},{4,8},{8,12},{12,16},{16,20},{20,24},{24,28},{1,5},{5,9},{9,... | collective-permute-start | bytes 2359304 | tf_op jit(solution)/shard_map/ppermute | solution.py:20
  59.4 27.0 %collective-permute-start.5 = (f32[12,32,512]{2,1,0:T(8,128)S(1)}, f32[12,32,512]{2,1,0:T(8,128)S(1)}, u32[]{:S(2)}, u32[]{:S(2)}) collective-permute-start(f32[12,32,512]{2,1,0:T(8,128)S(1)} %collective-permute-done.4.refs_21_.refs_2_), channel_id=1, source_target_pairs={{0,1},{1,0},{2,3},{3,2},{4,5},{5,4},{6,7},{7,6},{8,9},{9,8},{10,11... | collective-permute-start | bytes 2359304 | tf_op jit(solution)/shard_map/ppermute | solution.py:25
  59.5 1.1 copy-start.6
  79.7 6.7 %collective-permute-start.13 = (f32[12,32,512]{2,1,0:T(8,128)S(1)}, f32[12,32,512]{2,1,0:T(8,128)S(1)}, u32[]{:S(2)}, u32[]{:S(2)}) collective-permute-start(f32[12,32,512]{2,1,0:T(8,128)S(1)} %copied.9.refs_4_), channel_id=1, source_target_pairs={{0,1},{1,0},{2,3},{3,2},{4,5},{5,4},{6,7},{7,6},{8,9},{9,8},{10,11... | collective-permute-start | bytes 2359304 | tf_op jit(solution)/shard_map/ppermute | solution.py:25
  80.3 20.6 %collective-permute-start.19 = (f32[12,32,512]{2,1,0:T(8,128)S(1)}, f32[12,32,512]{2,1,0:T(8,128)S(1)}, u32[]{:S(2)}, u32[]{:S(2)}) collective-permute-start(f32[12,32,512]{2,1,0:T(8,128)S(1)} %copied.10.refs_2_), channel_id=1, source_target_pairs={{0,2},{1,3},{2,0},{3,1},{4,6},{5,7},{6,4},{7,5},{8,10},{9,11},{10,... | collective-permute-start | bytes 2359304 | tf_op jit(solution)/shard_map/ppermute | solution.py:25
  80.9 21.9 %collective-permute-start.23 = (f32[12,32,512]{2,1,0:T(8,128)S(1)}, f32[12,32,512]{2,1,0:T(8,128)S(1)}, u32[]{:S(2)}, u32[]{:S(2)}) collective-permute-start(f32[12,32,512]{2,1,0:T(8,128)S(1)} %get-tuple-element.41), channel_id=1, source_target_pairs={{0,4},{4,8},{8,12},{12,16},{16,20},{20,24},{24,28},{1,5},{5,9},{9,... | collective-permute-start | bytes 2359304 | tf_op jit(solution)/shard_map/ppermute | solution.py:20
  86.3 22.6 %collective-permute-start.18 = (f32[12,32,512]{2,1,0:T(8,128)S(1)}, f32[12,32,512]{2,1,0:T(8,128)S(1)}, u32[]{:S(2)}, u32[]{:S(2)}) collective-permute-start(f32[12,32,512]{2,1,0:T(8,128)S(1)} %copied.10.refs_2_), channel_id=1, source_target_pairs={{0,1},{1,0},{2,3},{3,2},{4,5},{5,4},{6,7},{7,6},{8,9},{9,8},{10,11... | collective-permute-start | bytes 2359304 | tf_op jit(solution)/shard_map/ppermute | solution.py:25
  101.0 8.4 %collective-permute-start.20 = (f32[12,32,512]{2,1,0:T(8,128)S(1)}, f32[12,32,512]{2,1,0:T(8,128)S(1)}, u32[]{:S(2)}, u32[]{:S(2)}) collective-permute-start(f32[12,32,512]{2,1,0:T(8,128)S(1)} %copied.11.refs_4_), channel_id=1, source_target_pairs={{0,1},{1,0},{2,3},{3,2},{4,5},{5,4},{6,7},{7,6},{8,9},{9,8},{10,11... | collective-permute-start | bytes 2359304 | tf_op jit(solution)/shard_map/ppermute | solution.py:25
  102.8 21.1 %collective-permute-start.25 = (f32[12,32,512]{2,1,0:T(8,128)S(1)}, f32[12,32,512]{2,1,0:T(8,128)S(1)}, u32[]{:S(2)}, u32[]{:S(2)}) collective-permute-start(f32[12,32,512]{2,1,0:T(8,128)S(1)} %copied.12.refs_2_), channel_id=1, source_target_pairs={{0,2},{1,3},{2,0},{3,1},{4,6},{5,7},{6,4},{7,5},{8,10},{9,11},{10,... | collective-permute-start | bytes 2359304 | tf_op jit(solution)/shard_map/ppermute | solution.py:25
  104.4 19.9 %collective-permute-start.29 = (f32[12,32,512]{2,1,0:T(8,128)S(1)}, f32[12,32,512]{2,1,0:T(8,128)S(1)}, u32[]{:S(2)}, u32[]{:S(2)}) collective-permute-start(f32[12,32,512]{2,1,0:T(8,128)S(1)} %get-tuple-element.44), channel_id=1, source_target_pairs={{0,4},{4,8},{8,12},{12,16},{16,20},{20,24},{24,28},{1,5},{5,9},{9,... | collective-permute-start | bytes 2359304 | tf_op jit(solution)/shard_map/ppermute | solution.py:20
  108.8 16.1 %collective-permute-start.14 = (f32[2,128,512]{2,1,0:T(8,128)S(1)}, f32[2,128,512]{2,1,0:T(8,128)S(1)}, u32[]{:S(2)}, u32[]{:S(2)}) collective-permute-start(f32[2,128,512]{2,1,0:T(8,128)S(1)} %get-tuple-element.38.refs_1_.refs_10_), channel_id=1, source_target_pairs={{0,1},{1,0},{2,3},{3,2},{4,5},{5,4},{6,7},{7,6},{8,9},{9,8},{10,11... | collective-permute-start | bytes 1572872 | tf_op jit(solution)/shard_map/ppermute | solution.py:25
  108.9 17.7 %collective-permute-start.24 = (f32[12,32,512]{2,1,0:T(8,128)S(1)}, f32[12,32,512]{2,1,0:T(8,128)S(1)}, u32[]{:S(2)}, u32[]{:S(2)}) collective-permute-start(f32[12,32,512]{2,1,0:T(8,128)S(1)} %copied.12.refs_2_), channel_id=1, source_target_pairs={{0,1},{1,0},{2,3},{3,2},{4,5},{5,4},{6,7},{7,6},{8,9},{9,8},{10,11... | collective-permute-start | bytes 2359304 | tf_op jit(solution)/shard_map/ppermute | solution.py:25
  124.0 3.1 %collective-permute-start.26 = (f32[12,32,512]{2,1,0:T(8,128)S(1)}, f32[12,32,512]{2,1,0:T(8,128)S(1)}, u32[]{:S(2)}, u32[]{:S(2)}) collective-permute-start(f32[12,32,512]{2,1,0:T(8,128)S(1)} %copied.13.refs_4_), channel_id=1, source_target_pairs={{0,1},{1,0},{2,3},{3,2},{4,5},{5,4},{6,7},{7,6},{8,9},{9,8},{10,11... | collective-permute-start | bytes 2359304 | tf_op jit(solution)/shard_map/ppermute | solution.py:25
  124.4 20.4 %collective-permute-start.31 = (f32[12,32,512]{2,1,0:T(8,128)S(1)}, f32[12,32,512]{2,1,0:T(8,128)S(1)}, u32[]{:S(2)}, u32[]{:S(2)}) collective-permute-start(f32[12,32,512]{2,1,0:T(8,128)S(1)} %copied.14.refs_2_), channel_id=1, source_target_pairs={{0,2},{1,3},{2,0},{3,1},{4,6},{5,7},{6,4},{7,5},{8,10},{9,11},{10,... | collective-permute-start | bytes 2359304 | tf_op jit(solution)/shard_map/ppermute | solution.py:25
  125.1 24.7 %collective-permute-start.15 = (f32[128,512]{1,0:T(8,128)S(1)}, f32[128,512]{1,0:T(8,128)S(1)}, u32[]{:S(2)}, u32[]{:S(2)}) collective-permute-start(f32[128,512]{1,0:T(8,128)S(1)} %get-tuple-element.49), channel_id=1, source_target_pairs={{0,2},{1,3},{2,0},{3,1},{4,6},{5,7},{6,4},{7,5},{8,10},{9,11},{10,... | collective-permute-start | bytes 786440 | tf_op jit(solution)/shard_map/ppermute | solution.py:25
  126.6 24.7 %collective-permute-start.21 = (f32[2,128,512]{2,1,0:T(8,128)S(1)}, f32[2,128,512]{2,1,0:T(8,128)S(1)}, u32[]{:S(2)}, u32[]{:S(2)}) collective-permute-start(f32[2,128,512]{2,1,0:T(8,128)S(1)} %get-tuple-element.40.refs_1_.refs_10_), channel_id=1, source_target_pairs={{0,1},{1,0},{2,3},{3,2},{4,5},{5,4},{6,7},{7,6},{8,9},{9,8},{10,11... | collective-permute-start | bytes 1572872 | tf_op jit(solution)/shard_map/ppermute | solution.py:25
  126.6 27.1 %collective-permute-start.30 = (f32[12,32,512]{2,1,0:T(8,128)S(1)}, f32[12,32,512]{2,1,0:T(8,128)S(1)}, u32[]{:S(2)}, u32[]{:S(2)}) collective-permute-start(f32[12,32,512]{2,1,0:T(8,128)S(1)} %copied.14.refs_2_), channel_id=1, source_target_pairs={{0,1},{1,0},{2,3},{3,2},{4,5},{5,4},{6,7},{7,6},{8,9},{9,8},{10,11... | collective-permute-start | bytes 2359304 | tf_op jit(solution)/shard_map/ppermute | solution.py:25
  144.8 8.9 %collective-permute-start.32 = (f32[12,32,512]{2,1,0:T(8,128)S(1)}, f32[12,32,512]{2,1,0:T(8,128)S(1)}, u32[]{:S(2)}, u32[]{:S(2)}) collective-permute-start(f32[12,32,512]{2,1,0:T(8,128)S(1)} %copied.15.refs_4_), channel_id=1, source_target_pairs={{0,1},{1,0},{2,3},{3,2},{4,5},{5,4},{6,7},{7,6},{8,9},{9,8},{10,11... | collective-permute-start | bytes 2359304 | tf_op jit(solution)/shard_map/ppermute | solution.py:25
  144.9 7.1 %collective-permute-start.27 = (f32[2,128,512]{2,1,0:T(8,128)S(1)}, f32[2,128,512]{2,1,0:T(8,128)S(1)}, u32[]{:S(2)}, u32[]{:S(2)}) collective-permute-start(f32[2,128,512]{2,1,0:T(8,128)S(1)} %get-tuple-element.43.refs_1_.refs_10_), channel_id=1, source_target_pairs={{0,1},{1,0},{2,3},{3,2},{4,5},{5,4},{6,7},{7,6},{8,9},{9,8},{10,11... | collective-permute-start | bytes 1572872 | tf_op jit(solution)/shard_map/ppermute | solution.py:25
  149.8 18.5 %collective-permute-start.16 = (f32[128,512]{1,0:T(8,128)S(1)}, f32[128,512]{1,0:T(8,128)S(1)}, u32[]{:S(2)}, u32[]{:S(2)}) collective-permute-start(f32[128,512]{1,0:T(8,128)S(1)} %added.3), channel_id=1, source_target_pairs={{4,0},{8,4},{12,8},{16,12},{20,16},{24,20},{28,24},{5,1},{9,5},{13... | collective-permute-start | bytes 786440 | tf_op jit(solution)/shard_map/ppermute | solution.py:20
  151.4 16.9 %collective-permute-start.22 = (f32[128,512]{1,0:T(8,128)S(1)}, f32[128,512]{1,0:T(8,128)S(1)}, u32[]{:S(2)}, u32[]{:S(2)}) collective-permute-start(f32[128,512]{1,0:T(8,128)S(1)} %get-tuple-element.53), channel_id=1, source_target_pairs={{0,2},{1,3},{2,0},{3,1},{4,6},{5,7},{6,4},{7,5},{8,10},{9,11},{10,... | collective-permute-start | bytes 786440 | tf_op jit(solution)/shard_map/ppermute | solution.py:25
  152.1 16.2 %collective-permute-start.28 = (f32[128,512]{1,0:T(8,128)S(1)}, f32[128,512]{1,0:T(8,128)S(1)}, u32[]{:S(2)}, u32[]{:S(2)}) collective-permute-start(f32[128,512]{1,0:T(8,128)S(1)} %get-tuple-element.51), channel_id=1, source_target_pairs={{0,2},{1,3},{2,0},{3,1},{4,6},{5,7},{6,4},{7,5},{8,10},{9,11},{10,... | collective-permute-start | bytes 786440 | tf_op jit(solution)/shard_map/ppermute | solution.py:25
  168.2 2.0 %collective-permute-start.34 = (f32[2,128,512]{2,1,0:T(8,128)S(1)}, f32[2,128,512]{2,1,0:T(8,128)S(1)}, u32[]{:S(2)}, u32[]{:S(2)}) collective-permute-start(f32[2,128,512]{2,1,0:T(8,128)S(1)} %get-tuple-element.45.refs_5_), channel_id=1, source_target_pairs={{0,1},{1,0},{2,3},{3,2},{4,5},{5,4},{6,7},{7,6},{8,9},{9,8},{10,11... | collective-permute-start | bytes 1572872 | tf_op jit(solution)/shard_map/ppermute | solution.py:25
  168.5 17.3 %collective-permute-start.33 = (f32[256,512]{1,0:T(8,128)S(1)}, f32[256,512]{1,0:T(8,128)S(1)}, u32[]{:S(2)}, u32[]{:S(2)}) collective-permute-start(f32[256,512]{1,0:T(8,128)S(1)} %pad_maximum_fusion), channel_id=1, source_target_pairs={{4,0},{8,4},{12,8},{16,12},{20,16},{24,20},{28,24},{5,1},{9,5},{13... | collective-permute-start | bytes 1572872 | tf_op jit(solution)/shard_map/ppermute | solution.py:20
  170.3 8.4 %collective-permute-start.35 = (f32[128,512]{1,0:T(8,128)S(1)}, f32[128,512]{1,0:T(8,128)S(1)}, u32[]{:S(2)}, u32[]{:S(2)}) collective-permute-start(f32[128,512]{1,0:T(8,128)S(1)} %get-tuple-element.55), channel_id=1, source_target_pairs={{0,2},{1,3},{2,0},{3,1},{4,6},{5,7},{6,4},{7,5},{8,10},{9,11},{10,... | collective-permute-start | bytes 786440 | tf_op jit(solution)/shard_map/ppermute | solution.py:25
  178.8 12.4 %collective-permute-start.36 = (f32[128,512]{1,0:T(8,128)S(1)}, f32[128,512]{1,0:T(8,128)S(1)}, u32[]{:S(2)}, u32[]{:S(2)}) collective-permute-start(f32[128,512]{1,0:T(8,128)S(1)} %added.5), channel_id=1, source_target_pairs={{4,0},{8,4},{12,8},{16,12},{20,16},{24,20},{28,24},{5,1},{9,5},{13... | collective-permute-start | bytes 786440 | tf_op jit(solution)/shard_map/ppermute | solution.py:20
